TPU v7x, 32 devices: a whole 2x2x4 slice. The times are simulated.
32 devices in a mesh: prow: 4 (over x, core), pcol: 8 (over z, y).
Axes of the slice: x: 2, y: 2, z: 4, core: 2. Of those that a mesh axis runs over, the one named last changes fastest.
Arguments:
- ancestor_inverse: float32 [2048, 2048], P('prow', 'pcol'), may hold values from -6 to 6
- block_mask: int32 [8, 8], replicated, may hold values 0 or 1
- block_ids: int32 [8], replicated, may hold values from 0 to 7, each once
- row_lists: int32 [4, 4], replicated, may hold values from 0 to 7, as said below
- panels: float32 [2048, 512], P(('prow', 'pcol')), may hold values from -0.21875 to 0.21875
- diag_inverse: float32 [4, 128, 128], replicated, may hold values from -6 to 6
Outputs:
- inverse_panels: float32 [2048, 512], P(('prow', 'pcol'))
- diag_blocks: float32 [4, 128, 128], replicated
Inputs may be any that keep to these rules, and one draw needn't show every extreme that they name: `row_lists`: each row names 4 different ancestor blocks.
All inputs are finite; a program needn't handle non-finite values.
Results may differ from a plain program's by a relative error of at most 0.0003.
Values sent between devices are 32-bit elements; how exact they have to be, the bound alone decides.
A program may use at most 64 MiB of HBM per device.

v0:
```python
import jax
import jax.numpy as jnp
from jax import lax
from jax.sharding import PartitionSpec as P

BLK = 256
W = 128
S = 4


def from_partner(block, axis, stride):
    count = lax.axis_size(axis)
    route = []
    for low in range(count):
        high = low | 1 << stride
        if high != low and high < count:
            route += [(low, high), (high, low)]
    return lax.ppermute(block, axis, route)


def local(ancestor_inverse, block_mask, block_ids, row_lists, panels, diag_inverse):
    row_devices = lax.axis_size("prow")
    col_devices = lax.axis_size("pcol")
    prow_index = lax.axis_index("prow")
    pcol_index = lax.axis_index("pcol")
    row_count = panels.shape[0]
    block_total = block_ids.shape[0]
    panel_width = S * W
    row_span = ancestor_inverse.shape[0]
    col_span = ancestor_inverse.shape[1]
    active_blocks = jnp.any(block_ids[:, None, None] == row_lists[None, :, :], axis=2).astype(
        jnp.float32
    )
    flat_index = prow_index * col_devices + pcol_index
    own_rows = flat_index * row_count + jnp.arange(row_count, dtype=jnp.int32)
    picker = (own_rows[:, None] // BLK == jnp.arange(block_total, dtype=jnp.int32)[None, :]).astype(
        jnp.float32
    )
    own_keep = jnp.repeat(
        jnp.dot(picker, active_blocks, preferred_element_type=jnp.float32), W, axis=1
    )
    active_own = panels * own_keep
    half_rows = row_count // 2
    upper_part = active_own[:half_rows]
    lower_part = active_own[half_rows:]
    in_first = pcol_index // row_devices == 0
    kept_part = jnp.where(in_first, upper_part, lower_part)
    given_part = jnp.where(in_first, lower_part, upper_part)
    pair_bit = row_devices.bit_length() - 1
    partner_part = from_partner(given_part, "pcol", pair_bit)
    stacked = jnp.stack([kept_part, partner_part])[None]
    colset = lax.all_gather(stacked, "prow", axis=0, tiled=True)
    send_slots = jnp.where(in_first, colset, colset[:, ::-1]).reshape(
        col_devices, half_rows, panel_width
    )
    arrived = lax.all_to_all(send_slots, "pcol", split_axis=0, concat_axis=0, tiled=True)
    needed = jnp.concatenate([arrived[:row_devices], arrived[row_devices:]], axis=1).reshape(
        col_span, panel_width
    )
    block_rows = row_span // BLK
    block_cols = col_span // BLK
    local_mask = lax.dynamic_slice(
        block_mask, (prow_index * block_rows, pcol_index * block_cols), (block_rows, block_cols)
    ).astype(jnp.float32)
    masked_local = (
        ancestor_inverse.reshape(block_rows, BLK, block_cols, BLK) * local_mask[:, None, :, None]
    ).reshape(row_span, col_span)
    partial_value = jnp.dot(
        masked_local, needed, precision=lax.Precision.HIGHEST, preferred_element_type=jnp.float32
    )
    summed = lax.psum_scatter(partial_value, "pcol", scatter_dimension=0, tiled=True)
    inverse_panels = -(own_keep * summed)
    local_diag = jnp.einsum(
        "isa,isb->sab",
        active_own.reshape(row_count, S, W),
        inverse_panels.reshape(row_count, S, W),
        precision=lax.Precision.HIGHEST,
    )
    diag_total = lax.psum(local_diag, ("prow", "pcol"))
    return (inverse_panels, diag_inverse - diag_total)


def solution(mesh):
    placed = (P("prow", "pcol"), P(), P(), P(), P(("prow", "pcol"), None), P())
    return jax.shard_map(
        local,
        mesh=mesh,
        in_specs=placed,
        out_specs=(P(("prow", "pcol"), None), P()),
        check_vma=False,
    )
```

profile of v0, /device:TPU:0, one launch (start us, length us, event | category | flops | bytes accessed | tf_op | source)
XLA Modules:
  0.0 249.5 jit_solution(15061585589461690380)
XLA Ops:
  7.2 0.0 copy-start.4
  7.2 0.0 copy-start.5
  7.2 0.0 copy-start.3
  7.2 0.6 copy-done.4
  7.9 0.0 copy-done.5
  7.9 0.1 compare_reduce_fusion
  7.9 0.2 fusion.9
  8.1 0.1 broadcast_in_dim.4
  8.3 0.0 copy-done.3
  8.3 4.1 %collective-permute-start = (f32[32,512]{1,0:T(8,128)S(1)}, f32[32,512]{1,0:T(8,128)S(1)}, u32[]{:S(2)}, u32[]{:S(2)}) collective-permute-start(f32[32,512]{1,0:T(8,128)S(1)} %get-tuple-element.5), channel_id=1, source_target_pairs={{0,4},{4,0},{1,5},{5,1},{2,6},{6,2},{3,7},{7,3},{8,12},{12,8},{9,1... | collective-permute-start | bytes 196616 | tf_op jit(solution)/shard_map/ppermute | solution.py:18
  12.4 3.6 %collective-permute-done = f32[32,512]{1,0:T(8,128)S(1)} collective-permute-done((f32[32,512]{1,0:T(8,128)S(1)}, f32[32,512]{1,0:T(8,128)S(1)}, u32[]{:S(2)}, u32[]{:S(2)}) %collective-permute-start) | collective-permute-done | bytes 65568 | tf_op jit(solution)/shard_map/ppermute | solution.py:18
  16.1 7.4 %all-gather = f32[8,32,512]{2,1,0:T(8,128)S(1)} all-gather(f32[2,32,512]{2,1,0:T(8,128)S(1)} %pad_maximum_fusion.1), channel_id=2, replica_groups=mesh['prow'=4,'pcol'=8] {'prow'}, dimensions={0}, use_global_device_ids=true | all-gather | bytes 655360 | tf_op jit(solution)/shard_map/all_gather | solution.py:52
  23.5 0.8 reverse_select_fusion
  24.3 5.4 %all-to-all-start = ((f32[8,32,512]{2,1,0:T(8,128)}), f32[8,32,512]{2,1,0:T(8,128)S(1)}, u32[]{:S(2)}, u32[]{:S(2)}) async-start(f32[8,32,512]{2,1,0:T(8,128)} %bitcast.3), calls=%async_computation | async-start | bytes 1048576 | tf_op jit(solution)/shard_map/all_to_all | solution.py:56
  29.7 0.0 reduce-scatter.2.cloned.1.call-start
  29.8 0.9 convert_reduce_fusion
  30.6 0.1 broadcast_bitcast_fusion
  30.7 14.0 %all-to-all-done = f32[8,32,512]{2,1,0:T(8,128)S(1)} async-done(((f32[8,32,512]{2,1,0:T(8,128)}), f32[8,32,512]{2,1,0:T(8,128)S(1)}, u32[]{:S(2)}, u32[]{:S(2)}) %all-to-all-start) | async-done | bytes 524320 | tf_op jit(solution)/shard_map/all_to_all | solution.py:56
  44.8 0.0 copy-start
  44.8 1.0 copy-done
  45.8 2.0 fusion
  47.8 0.0 reduce-scatter.2.cloned.1.call-update
  47.8 0.0 all-reduce.2.cloned.1.call-start
  47.9 62.1 %reduce-scatter.2.cloned.1.call-done = f32[64,512]{1,0:T(8,128)} async-done(((f32[512,512]{1,0:T(8,128)}), f32[64,512]{1,0:T(8,128)}) %reduce-scatter.2.cloned.1.call-update) | async-done | bytes 131088 | tf_op jit(solution)/shard_map/reduce_scatter | solution.py:71
  110.0 0.9 fusion.3
  110.9 0.0 copy-start.1
  110.9 1.3 fusion.4
  112.2 0.0 copy-done.1
  112.2 0.0 copy-start.2
  112.2 0.0 all-reduce.2.cloned.1.call-update
  112.2 128.8 %all-reduce.2.cloned.1.call-done = f32[4,128,128]{2,1,0:T(8,128)} async-done(((f32[4,128,128]{2,1,0:T(8,128)}), f32[4,128,128]{2,1,0:T(8,128)}) %all-reduce.2.cloned.1.call-update) | async-done | bytes 262160 | tf_op jit(solution)/shard_map/psum | solution.py:79
  241.0 0.0 copy-done.2
  241.0 1.7 sub.15
  (7 shorter events, 0.1 us)
Async XLA Ops:
  7.2 0.7 copy-start.4
  7.2 0.7 copy-start.5
  7.2 1.1 copy-start.3
  8.3 7.8 %collective-permute-start = (f32[32,512]{1,0:T(8,128)S(1)}, f32[32,512]{1,0:T(8,128)S(1)}, u32[]{:S(2)}, u32[]{:S(2)}) collective-permute-start(f32[32,512]{1,0:T(8,128)S(1)} %get-tuple-element.5), channel_id=1, source_target_pairs={{0,4},{4,0},{1,5},{5,1},{2,6},{6,2},{3,7},{7,3},{8,12},{12,8},{9,1... | collective-permute-start | bytes 196616 | tf_op jit(solution)/shard_map/ppermute | solution.py:18
  24.3 20.4 %all-to-all-start = ((f32[8,32,512]{2,1,0:T(8,128)}), f32[8,32,512]{2,1,0:T(8,128)S(1)}, u32[]{:S(2)}, u32[]{:S(2)}) async-start(f32[8,32,512]{2,1,0:T(8,128)} %bitcast.3), calls=%async_computation | async-start | bytes 1048576 | tf_op jit(solution)/shard_map/all_to_all | solution.py:56
  29.7 80.2 %reduce-scatter.2.cloned.1.call-start = ((), (), s32[]{:S(2)}) async-start(), calls=%async_computation.2 | async-start | bytes 1179648 | tf_op jit(solution)/shard_map/reduce_scatter | solution.py:71
  44.8 1.0 copy-start
  47.8 193.1 %all-reduce.2.cloned.1.call-start = ((), (), s32[]{:S(2)}) async-start(), calls=%async_computation.3 | async-start | bytes 524288 | tf_op jit(solution)/shard_map/psum | solution.py:79
  110.9 1.3 copy-start.1
  112.2 128.8 %copy-start.2 = (f32[4,128,128]{2,1,0:T(8,128)S(1)}, f32[4,128,128]{2,1,0:T(8,128)}, u32[]{:S(2)}) copy-start(f32[4,128,128]{2,1,0:T(8,128)} %param.11) | copy-start | bytes 786436
Sparse Core Ops, SparseCore 0:
  48.0 61.9 reduce-scatter.1
  116.9 124.0 all-reduce.1
where the time goes:
time: 250 us
  waiting for transfers between devices  209 us (84%)
  between operations  14.2 us (6%)
  starting transfers between devices  9.59 us (4%)
  blocking collectives  7.38 us (3%)
  other arithmetic  4.5 us (2%)
  matrix products  3.5 us (1%)
    psum x1, waiting for transfers between devices, local(): diag_total = lax.psum(local_diag, ('prow', 'pcol'))  129 us
    reduce_scatter x1, waiting for transfers between devices, local(): lax.psum_scatter(partial_value, 'pcol', scatter_dimension=0, tiled=True)  62.1 us
    all_to_all x1, waiting for transfers between devices, local(): lax.all_to_all(send_slots, 'pcol', split_axis=0, concat_axis=0, tiled=True)  14 us
    all_gather x1, blocking collectives, local(): colset = lax.all_gather(stacked, 'prow', axis=0, tiled=True)  7.38 us
    all_to_all x1, starting transfers between devices, local(): lax.all_to_all(send_slots, 'pcol', split_axis=0, concat_axis=0, tiled=True)  5.41 us
  transfers between devices with their start and end apart: 4, of which 4 were waited for; matrix products, arithmetic and copies ran while one was open for 0% of the time, Pallas kernels for 0%

commit v1 on v0

--- a/solution.py
+++ b/solution.py
@@ -1,11 +1,387 @@
+import functools
+import itertools
+
 import jax
 import jax.numpy as jnp
 from jax import lax
+from jax.experimental import pallas as pl
+from jax.experimental.pallas import tpu as pltpu
 from jax.sharding import PartitionSpec as P
 
 BLK = 256
 W = 128
 S = 4
+CHUNKS = 4
+CORES = 2
+MESH = pl.DeviceIdType.MESH
+
+
+def halves(value):
+    high = value.astype(jnp.bfloat16)
+    low = (value - high.astype(jnp.float32)).astype(jnp.bfloat16)
+    return high, low
+
+
+def dot3(a_high, a_low, b_high, b_low):
+    dot = functools.partial(jnp.dot, preferred_element_type=jnp.float32)
+    return dot(a_high, b_low) + dot(a_low, b_high) + dot(a_high, b_high)
+
+
+def fused(
+    rows_n,
+    cols_n,
+    block_mask,
+    block_ids,
+    row_lists,
+    ancestor,
+    panels,
+    diag_inverse,
+    panels_out,
+    diag_out,
+    act,
+    far_cols,
+    a_high,
+    a_low,
+    needed,
+    partial,
+    arrived,
+    diag_local,
+    diag_near,
+    diag_line,
+    diag_all,
+    sem_a,
+    send_1,
+    recv_1,
+    send_2,
+    recv_2,
+    sem_3,
+    send_c,
+    recv_c,
+    send_d1,
+    recv_d1,
+    send_d2,
+    recv_d2,
+    send_d3,
+    recv_d3,
+):
+    r = lax.axis_index("prow")
+    c = lax.axis_index("pcol")
+    q = c // 2
+    h = c % 2
+    x = r // CORES
+    core = r % CORES
+    far_h = 1 - h
+    m = panels.shape[0]
+    piece = m // rows_n
+    row_span = rows_n * 2 * m
+    chunks = act.shape[0]
+    per_chunk = S // chunks
+    plane = rows_n * 2
+    nr = row_lists.shape[1]
+
+    barrier = pltpu.get_barrier_semaphore()
+    total = rows_n * cols_n
+    flat = r * cols_n + c
+    for step in range(1, total):
+        other = lax.rem(flat + step, total)
+        pl.semaphore_signal(
+            barrier, inc=1, device_id=(other // cols_n, other % cols_n), device_id_type=MESH
+        )
+
+    def active(block, k):
+        hit = block_ids[block] == row_lists[k, 0]
+        for n in range(1, nr):
+            hit = jnp.logical_or(hit, block_ids[block] == row_lists[k, n])
+        return jnp.where(hit, 1.0, 0.0).astype(jnp.float32)
+
+    own_block = (flat * m) // BLK
+    keep = [active(own_block, k) for k in range(S)]
+    for k in range(S):
+        g, i = divmod(k, per_chunk)
+        act[g, :, i * W : (i + 1) * W] = panels[:, k * W : (k + 1) * W] * keep[k]
+
+    pl.semaphore_wait(barrier, total - 1)
+
+    def remote(src, dst, send, recv, device):
+        return pltpu.make_async_remote_copy(
+            src_ref=src, dst_ref=dst, send_sem=send, recv_sem=recv, device_id=device, device_id_type=MESH
+        )
+
+    pending = []
+
+    def first(g, j):
+        to = lax.rem(r + j, rows_n)
+        return remote(
+            act.at[g, pl.ds(to * piece, piece)],
+            needed.at[g, q, h, to // CORES, to % CORES],
+            send_1.at[g, j],
+            recv_1.at[g, q],
+            (to, r * 2 + h),
+        )
+
+    for g in range(chunks):
+        for j in range(1, rows_n):
+            copy = first(g, j)
+            copy.start()
+            pending.append(copy)
+
+        @pl.when(q != r)
+        def _():
+            first(g, 0).start()
+
+        @pl.when(q == r)
+        def _():
+            needed[g, q, h, x, core] = act[g, pl.ds(r * piece, piece)]
+
+    swap = remote(ancestor.at[:, far_h], far_cols, sem_a.at[0], sem_a.at[1], (r, 2 * q + far_h))
+    swap.start()
+    pending.append(swap)
+
+    near_steps = [(dx, dh) for dx in range(rows_n // CORES) for dh in range(2)][1:]
+    plane_steps = [(dr, dh) for dr in range(rows_n) for dh in range(2)][1:]
+    copies = {}
+
+    def split_rows(source, slot, column):
+        for to in range(rows_n):
+            block = (r * row_span + (2 * to + h) * m) // BLK
+            keep_block = block_mask[block, column].astype(jnp.float32)
+            high, low = halves(source[to] * keep_block)
+            a_high[slot, to * m : (to + 1) * m] = high
+            a_low[slot, to * m : (to + 1) * m] = low
+
+    def second(g):
+        for source in range(rows_n):
+            wait = remote(
+                act.at[g, pl.ds(0, piece)],
+                needed.at[g, source, h, x, core],
+                send_1.at[g, 0],
+                recv_1.at[g, source],
+                (r, c),
+            )
+
+            @pl.when(jnp.logical_or(q != source, r != source))
+            def _():
+                wait.wait_recv()
+
+        for j, (dx, dh) in enumerate(near_steps):
+            to_x = lax.rem(x + dx, rows_n // CORES)
+            to_h = lax.rem(h + dh, 2)
+            block = needed.at[g, :, h, x, core]
+            copy = remote(
+                block, block, send_2.at[g, j], recv_2.at[g, j], (to_x * CORES + core, 2 * q + to_h)
+            )
+            copy.start()
+            pending.append(copy)
+            copies["second", g, j] = copy
+
+    def third(g):
+        for j, (dx, dh) in enumerate(near_steps):
+            from_x = lax.rem(x - dx + rows_n // CORES, rows_n // CORES)
+            from_h = lax.rem(h - dh + 2, 2)
+            block = needed.at[g, :, from_h, from_x, core]
+            remote(block, block, send_2.at[g, j], recv_2.at[g, j], (r, c)).wait_recv()
+        block = needed.at[g, :, :, :, core]
+        copy = remote(
+            block, block, sem_3.at[0, g], sem_3.at[1, g], (x * CORES + 1 - core, c)
+        )
+        copy.start()
+        pending.append(copy)
+
+    def multiply(g):
+        if g == 0:
+            split_rows([ancestor[to, h] for to in range(rows_n)], h, c)
+            swap.wait_recv()
+            split_rows([far_cols[to] for to in range(rows_n)], far_h, 2 * q + far_h)
+        block = needed.at[g, :, :, :, 1 - core]
+        remote(block, block, sem_3.at[0, g], sem_3.at[1, g], (r, c)).wait_recv()
+        value = None
+        width = per_chunk * W
+        for side in range(2):
+            half = rows_n // 2
+            b_high, b_low = halves(
+                needed[g, side * half : (side + 1) * half].reshape(half * 2 * m, width)
+            )
+            term = dot3(a_high[side], a_low[side], b_high, b_low)
+            value = term if value is None else value + term
+        partial[g] = value.reshape(rows_n, m, width)
+        for j in range(1, rows_n):
+            to = lax.rem(q + j, rows_n)
+            copy = remote(
+                partial.at[g, to],
+                arrived.at[g, j - 1],
+                send_c.at[g, j - 1],
+                recv_c.at[g, j - 1],
+                (r, 2 * to + h),
+            )
+            copy.start()
+            pending.append(copy)
+            copies["line", g, j] = copy
+
+    def finish(g):
+        summed = partial[g, q]
+        for j in range(1, rows_n):
+            copies["line", g, j].wait_recv()
+            summed = summed + arrived[g, j - 1]
+        for i in range(per_chunk):
+            k = g * per_chunk + i
+            cols = slice(i * W, (i + 1) * W)
+            inverse = -(keep[k] * summed[:, cols])
+            panels_out[:, k * W : (k + 1) * W] = inverse
+            t_high, t_low = halves(act[g, :, cols].T)
+            i_high, i_low = halves(inverse)
+            diag_local[g, :, i] = dot3(t_high, t_low, i_high, i_low).reshape(plane, W // plane, W)
+        for j, (dr, dh) in enumerate(plane_steps):
+            to_r = lax.rem(r + dr, rows_n)
+            to_h = lax.rem(h + dh, 2)
+            copy = remote(
+                diag_local.at[g, to_r * 2 + to_h],
+                diag_near.at[g, j],
+                send_d1.at[g, j],
+                recv_d1.at[g, j],
+                (to_r, 2 * q + to_h),
+            )
+            copy.start()
+            pending.append(copy)
+            copies["d1", g, j] = copy
+
+    mine = r * 2 + h
+
+    def line_sum(g):
+        value = diag_local[g, mine]
+        for j in range(plane - 1):
+            copies["d1", g, j].wait_recv()
+            value = value + diag_near[g, j]
+        diag_line[g, q] = value
+        for j in range(1, rows_n):
+            to = lax.rem(q + j, rows_n)
+            copy = remote(
+                diag_line.at[g, q],
+                diag_line.at[g, q],
+                send_d2.at[g, j - 1],
+                recv_d2.at[g, j - 1],
+                (r, 2 * to + h),
+            )
+            copy.start()
+            pending.append(copy)
+
+    def spread(g):
+        for j in range(1, rows_n):
+            source = lax.rem(q - j + rows_n, rows_n)
+            remote(
+                diag_line.at[g, source],
+                diag_line.at[g, source],
+                send_d2.at[g, j - 1],
+                recv_d2.at[g, j - 1],
+                (r, c),
+            ).wait_recv()
+        value = diag_line[g, 0]
+        for source in range(1, rows_n):
+            value = value + diag_line[g, source]
+        share = W // plane
+        for i in range(per_chunk):
+            k = g * per_chunk + i
+            diag_all[g, mine, i] = diag_inverse[k, pl.ds(mine * share, share)] - value[i]
+        for j, (dr, dh) in enumerate(plane_steps):
+            to_r = lax.rem(r + dr, rows_n)
+            to_h = lax.rem(h + dh, 2)
+            copy = remote(
+                diag_all.at[g, mine],
+                diag_all.at[g, mine],
+                send_d3.at[g, j],
+                recv_d3.at[g, j],
+                (to_r, 2 * q + to_h),
+            )
+            copy.start()
+            pending.append(copy)
+
+    def store(g):
+        for j, (dr, dh) in enumerate(plane_steps):
+            source = lax.rem(r - dr + rows_n, rows_n) * 2 + lax.rem(h - dh + 2, 2)
+            remote(
+                diag_all.at[g, source],
+                diag_all.at[g, source],
+                send_d3.at[g, j],
+                recv_d3.at[g, j],
+                (r, c),
+            ).wait_recv()
+        for i in range(per_chunk):
+            diag_out[g * per_chunk + i] = diag_all[g, :, i].reshape(W, W)
+
+    stages = [second, third, multiply, finish, line_sum, spread, store]
+    for turn in range(chunks + len(stages) - 1):
+        for depth, stage in enumerate(stages):
+            if 0 <= turn - depth < chunks:
+                stage(turn - depth)
+
+    for copy in pending:
+        copy.wait_send()
+    for g in range(chunks):
+
+        @pl.when(q != r)
+        def _():
+            first(g, 0).wait_send()
+
+
+def planned(ancestor_inverse, block_mask, block_ids, row_lists, panels, diag_inverse):
+    rows_n = lax.axis_size("prow")
+    cols_n = lax.axis_size("pcol")
+    m = panels.shape[0]
+    col_span = ancestor_inverse.shape[1]
+    g = CHUNKS
+    width = S // g * W
+    plane = 2 * rows_n
+    piece = m // rows_n
+    share = W // plane
+    f32 = jnp.float32
+    dma = pltpu.SemaphoreType.DMA
+    vmem = pl.BlockSpec(memory_space=pltpu.VMEM)
+    smem = pl.BlockSpec(memory_space=pltpu.SMEM)
+    return pl.pallas_call(
+        functools.partial(fused, rows_n, cols_n),
+        out_shape=(
+            jax.ShapeDtypeStruct(panels.shape, f32),
+            jax.ShapeDtypeStruct(diag_inverse.shape, f32),
+        ),
+        in_specs=[smem, smem, smem, vmem, vmem, vmem],
+        out_specs=(vmem, vmem),
+        scratch_shapes=[
+            pltpu.VMEM((g, m, width), f32),
+            pltpu.VMEM((rows_n, m, col_span), f32),
+            pltpu.VMEM((2, rows_n * m, col_span), jnp.bfloat16),
+            pltpu.VMEM((2, rows_n * m, col_span), jnp.bfloat16),
+            pltpu.VMEM((g, rows_n, 2, rows_n // CORES, CORES, piece, width), f32),
+            pltpu.VMEM((g, rows_n, m, width), f32),
+            pltpu.VMEM((g, rows_n - 1, m, width), f32),
+            pltpu.VMEM((g, plane, S // g, share, W), f32),
+            pltpu.VMEM((g, plane - 1, S // g, share, W), f32),
+            pltpu.VMEM((g, rows_n, S // g, share, W), f32),
+            pltpu.VMEM((g, plane, S // g, share, W), f32),
+            dma((2,)),
+            dma((g, rows_n)),
+            dma((g, rows_n)),
+            dma((g, rows_n - 1)),
+            dma((g, rows_n - 1)),
+            dma((2, g)),
+            dma((g, rows_n - 1)),
+            dma((g, rows_n - 1)),
+            dma((g, plane - 1)),
+            dma((g, plane - 1)),
+            dma((g, rows_n - 1)),
+            dma((g, rows_n - 1)),
+            dma((g, plane - 1)),
+            dma((g, plane - 1)),
+        ],
+        compiler_params=pltpu.CompilerParams(
+            collective_id=0, has_side_effects=True, vmem_limit_bytes=32 * 1024 * 1024
+        ),
+    )(
+        block_mask,
+        block_ids,
+        row_lists,
+        ancestor_inverse.reshape(rows_n, 2, m, col_span),
+        panels,
+        diag_inverse,
+    )
 
 
 def from_partner(block, axis, stride):
@@ -18,7 +394,7 @@
     return lax.ppermute(block, axis, route)
 
 
-def local(ancestor_inverse, block_mask, block_ids, row_lists, panels, diag_inverse):
+def general(ancestor_inverse, block_mask, block_ids, row_lists, panels, diag_inverse):
     row_devices = lax.axis_size("prow")
     col_devices = lax.axis_size("pcol")
     prow_index = lax.axis_index("prow")
@@ -80,6 +456,22 @@
     return (inverse_panels, diag_inverse - diag_total)
 
 
+def local(ancestor_inverse, block_mask, block_ids, row_lists, panels, diag_inverse):
+    rows_n = lax.axis_size("prow")
+    cols_n = lax.axis_size("pcol")
+    m = panels.shape[0]
+    fits = (
+        cols_n == 2 * rows_n
+        and rows_n % CORES == 0
+        and m % (8 * rows_n) == 0
+        and BLK % m == 0
+        and ancestor_inverse.shape[1] == BLK
+        and W % (16 * rows_n) == 0
+    )
+    plan = planned if fits else general
+    return plan(ancestor_inverse, block_mask, block_ids, row_lists, panels, diag_inverse)
+
+
 def solution(mesh):
     placed = (P("prow", "pcol"), P(), P(), P(), P(("prow", "pcol"), None), P())
     return jax.shard_map(

time: 250 us -> 54.4 us (0.22)
  waiting for transfers between devices: 209 us -> 0 us
  Pallas kernels: 0 us -> 47.2 us
  between operations: 14.2 us -> 0.65 us
  starting transfers between devices: 9.59 us -> 0 us
  blocking collectives: 7.38 us -> 0 us
  other arithmetic: 4.5 us -> 0 us
  local copies, waits for them, and re-layouts: 1.87 us -> 6.27 us
  matrix products: 3.5 us -> 0 us
    psum x1 -> x0, waiting for transfers between devices: 129 us -> none  [local(): diag_total = lax.psum(local_diag, ('prow', 'pcol'))]
    reduce_scatter x1 -> x0, waiting for transfers between devices: 62.1 us -> none  [local(): lax.psum_scatter(partial_value, 'pcol', scatter_dimension=0, tiled=True)]
    pallas_call x0 -> x1, Pallas kernels: none -> 47.2 us  [planned(): pl.pallas_call(functools.partial(fused, rows_n, cols_n), out_shape=(jax.S...]
    all_to_all x1 -> x0, waiting for transfers between devices: 14 us -> none  [local(): lax.all_to_all(send_slots, 'pcol', split_axis=0, concat_axis=0, tiled=True)]
    all_gather x1 -> x0, blocking collectives: 7.38 us -> none  [local(): colset = lax.all_gather(stacked, 'prow', axis=0, tiled=True)]
    all_to_all x1 -> x0, starting transfers between devices: 5.41 us -> none  [local(): lax.all_to_all(send_slots, 'pcol', split_axis=0, concat_axis=0, tiled=True)]
    unnamed x14, local copies, waits for them, and re-layouts: 1.71 us -> 6.27 us
    ppermute x1 -> x0, starting transfers between devices: 4.1 us -> none  [from_partner(): return lax.ppermute(block, axis, route)]
  transfers between devices with their start and end apart: 4 -> 0, of which waited for: 4 -> 0; matrix products, arithmetic and copies ran while one was open for 0% -> 0% of each run, Pallas kernels for 0% -> 0%
where the time goes in v1:
time: 54.4 us; the launch traced here: 54.1 us
  Pallas kernels  47.2 us (87%)
  local copies, waits for them, and re-layouts  6.27 us (12%)
  between operations  0.65 us (1%)
    pallas_call x1, Pallas kernels, planned(): pl.pallas_call(functools.partial(fused, rows_n, cols_n), out_shape=(jax.S...  47.2 us
    unnamed x14, local copies, waits for them, and re-layouts  6.27 us

profile of v1, /device:TPU:0, one launch (start us, length us, event | category | flops | bytes accessed | tf_op | source)
XLA Modules:
  0.0 54.1 jit_solution(7045408437943475187)
XLA Ops:
  0.6 0.0 copy-start.5
  0.6 0.6 %copy-done.5 = s32[8]{0:T(128)S(1)} copy-done((s32[8]{0:T(128)S(1)}, s32[8]{0:T(128)}, u32[]{:S(2)}) %copy-start.5) | copy-done | bytes 56
  1.3 0.0 copy-start
  1.3 1.0 %copy-done = f32[512,256]{1,0:T(8,128)S(1)} copy-done((f32[512,256]{1,0:T(8,128)S(1)}, f32[512,256]{1,0:T(8,128)}, u32[]{:S(2)}) %copy-start) | copy-done | bytes 524312
  2.3 0.0 copy-start.1
  2.3 0.9 %copy-done.1 = f32[4,128,128]{2,1,0:T(8,128)S(1)} copy-done((f32[4,128,128]{2,1,0:T(8,128)S(1)}, f32[4,128,128]{2,1,0:T(8,128)}, u32[]{:S(2)}) %copy-start.1) | copy-done | bytes 262168
  3.3 0.0 copy-start.2
  3.3 0.9 %copy-done.2 = f32[64,512]{1,0:T(8,128)S(1)} copy-done((f32[64,512]{1,0:T(8,128)S(1)}, f32[64,512]{1,0:T(8,128)}, u32[]{:S(2)}) %copy-start.2) | copy-done | bytes 131096
  4.2 0.0 copy-start.3
  4.2 0.7 %copy-done.3 = s32[8,8]{1,0:T(8,128)S(1)} copy-done((s32[8,8]{1,0:T(8,128)S(1)}, s32[8,8]{1,0:T(8,128)}, u32[]{:S(2)}) %copy-start.3) | copy-done | bytes 280
  4.9 0.0 copy-start.4
  4.9 0.7 %copy-done.4 = s32[4,4]{1,0:T(4,128)S(1)} copy-done((s32[4,4]{1,0:T(4,128)S(1)}, s32[4,4]{1,0:T(4,128)}, u32[]{:S(2)}) %copy-start.4) | copy-done | bytes 88
  5.6 47.2 %shard_map.77 = (f32[64,512]{1,0:T(8,128)S(1)}, f32[4,128,128]{2,1,0:T(8,128)S(1)}) custom-call(s32[8,8]{1,0:T(8,128)S(1)} %copy-done.3, s32[8]{0:T(128)S(1)} %copy-done.5, s32[4,4]{1,0:T(4,128)S(1)} %copy-done.4, f32[4,2,64,256]{3,2,1,0:T(8,128)S(1)} %bitcast.1, f32[64,512]{1,0:T(8,128)S(1)} %copy-done.2, f32[4,128,128]{2,1,0:T(8,128)S(1)} %copy-done.1), custom_call_target="tpu_custom_call" | custom-call | tf_op jit(solution)/shard_map/pallas_call | solution.py:339
  52.8 0.7 %copy.10 = f32[64,512]{1,0:T(8,128)} copy(f32[64,512]{1,0:T(8,128)S(1)} %get-tuple-element.4) | data formatting | bytes 262144
  53.4 0.7 %copy.11 = f32[4,128,128]{2,1,0:T(8,128)} copy(f32[4,128,128]{2,1,0:T(8,128)S(1)} %get-tuple-element.5) | data formatting | bytes 524288
Async XLA Ops:
  0.6 0.7 %copy-start.5 = (s32[8]{0:T(128)S(1)}, s32[8]{0:T(128)}, u32[]{:S(2)}) copy-start(s32[8]{0:T(128)} %block_ids.1) | copy-start | bytes 100
  1.3 1.0 %copy-start = (f32[512,256]{1,0:T(8,128)S(1)}, f32[512,256]{1,0:T(8,128)}, u32[]{:S(2)}) copy-start(f32[512,256]{1,0:T(8,128)} %param.6) | copy-start | bytes 1572868
  2.3 0.9 %copy-start.1 = (f32[4,128,128]{2,1,0:T(8,128)S(1)}, f32[4,128,128]{2,1,0:T(8,128)}, u32[]{:S(2)}) copy-start(f32[4,128,128]{2,1,0:T(8,128)} %diag_inverse.1) | copy-start | bytes 786436
  3.3 0.9 %copy-start.2 = (f32[64,512]{1,0:T(8,128)S(1)}, f32[64,512]{1,0:T(8,128)}, u32[]{:S(2)}) copy-start(f32[64,512]{1,0:T(8,128)} %panels.1) | copy-start | bytes 393220
  4.2 0.7 %copy-start.3 = (s32[8,8]{1,0:T(8,128)S(1)}, s32[8,8]{1,0:T(8,128)}, u32[]{:S(2)}) copy-start(s32[8,8]{1,0:T(8,128)} %block_mask.1) | copy-start | bytes 772
  4.9 0.7 %copy-start.4 = (s32[4,4]{1,0:T(4,128)S(1)}, s32[4,4]{1,0:T(4,128)}, u32[]{:S(2)}) copy-start(s32[4,4]{1,0:T(4,128)} %row_lists.1) | copy-start | bytes 196

commit v2 on v1

--- a/solution.py
+++ b/solution.py
@@ -1,5 +1,4 @@
 import functools
-import itertools
 
 import jax
 import jax.numpy as jnp
@@ -11,7 +10,7 @@
 BLK = 256
 W = 128
 S = 4
-CHUNKS = 4
+CHUNKS = 2
 CORES = 2
 MESH = pl.DeviceIdType.MESH
 
@@ -30,14 +29,21 @@
 def fused(
     rows_n,
     cols_n,
+    mask_hbm,
+    ids_hbm,
+    lists_hbm,
+    ancestor,
+    panels_hbm,
+    diag_hbm,
+    panels_out,
+    diag_out,
     block_mask,
     block_ids,
     row_lists,
-    ancestor,
+    near_cols,
     panels,
     diag_inverse,
-    panels_out,
-    diag_out,
+    sem_in,
     act,
     far_cols,
     a_high,
@@ -79,6 +85,24 @@
     plane = rows_n * 2
     nr = row_lists.shape[1]
 
+    share = W // plane
+    mine = r * 2 + h
+    loads = [
+        pltpu.make_async_copy(src, dst, sem_in.at[i])
+        for i, (src, dst) in enumerate(
+            [
+                (panels_hbm, panels),
+                (ids_hbm, block_ids),
+                (lists_hbm, row_lists),
+                (mask_hbm, block_mask),
+                (ancestor.at[:, h], near_cols),
+                (diag_hbm.at[:, pl.ds(mine * share, share)], diag_inverse),
+            ]
+        )
+    ]
+    for load in loads:
+        load.start()
+
     barrier = pltpu.get_barrier_semaphore()
     total = rows_n * cols_n
     flat = r * cols_n + c
@@ -94,6 +118,8 @@
             hit = jnp.logical_or(hit, block_ids[block] == row_lists[k, n])
         return jnp.where(hit, 1.0, 0.0).astype(jnp.float32)
 
+    for load in loads[:4]:
+        load.wait()
     own_block = (flat * m) // BLK
     keep = [active(own_block, k) for k in range(S)]
     for k in range(S):
@@ -189,7 +215,8 @@
 
     def multiply(g):
         if g == 0:
-            split_rows([ancestor[to, h] for to in range(rows_n)], h, c)
+            loads[4].wait()
+            split_rows([near_cols[to] for to in range(rows_n)], h, c)
             swap.wait_recv()
             split_rows([far_cols[to] for to in range(rows_n)], far_h, 2 * q + far_h)
         block = needed.at[g, :, :, :, 1 - core]
@@ -244,8 +271,6 @@
             pending.append(copy)
             copies["d1", g, j] = copy
 
-    mine = r * 2 + h
-
     def line_sum(g):
         value = diag_local[g, mine]
         for j in range(plane - 1):
@@ -277,10 +302,10 @@
         value = diag_line[g, 0]
         for source in range(1, rows_n):
             value = value + diag_line[g, source]
-        share = W // plane
+        if g == 0:
+            loads[5].wait()
         for i in range(per_chunk):
-            k = g * per_chunk + i
-            diag_all[g, mine, i] = diag_inverse[k, pl.ds(mine * share, share)] - value[i]
+            diag_all[g, mine, i] = diag_inverse[g * per_chunk + i] - value[i]
         for j, (dr, dh) in enumerate(plane_steps):
             to_r = lax.rem(r + dr, rows_n)
             to_h = lax.rem(h + dh, 2)
@@ -335,16 +360,23 @@
     f32 = jnp.float32
     dma = pltpu.SemaphoreType.DMA
     vmem = pl.BlockSpec(memory_space=pltpu.VMEM)
-    smem = pl.BlockSpec(memory_space=pltpu.SMEM)
+    anywhere = pl.BlockSpec(memory_space=pl.ANY)
     return pl.pallas_call(
         functools.partial(fused, rows_n, cols_n),
         out_shape=(
             jax.ShapeDtypeStruct(panels.shape, f32),
             jax.ShapeDtypeStruct(diag_inverse.shape, f32),
         ),
-        in_specs=[smem, smem, smem, vmem, vmem, vmem],
+        in_specs=[anywhere] * 6,
         out_specs=(vmem, vmem),
         scratch_shapes=[
+            pltpu.SMEM(block_mask.shape, jnp.int32),
+            pltpu.SMEM(block_ids.shape, jnp.int32),
+            pltpu.SMEM(row_lists.shape, jnp.int32),
+            pltpu.VMEM((rows_n, m, col_span), f32),
+            pltpu.VMEM(panels.shape, f32),
+            pltpu.VMEM((S, share, W), f32),
+            dma((6,)),
             pltpu.VMEM((g, m, width), f32),
             pltpu.VMEM((rows_n, m, col_span), f32),
             pltpu.VMEM((2, rows_n * m, col_span), jnp.bfloat16),
@@ -372,7 +404,7 @@
             dma((g, plane - 1)),
         ],
         compiler_params=pltpu.CompilerParams(
-            collective_id=0, has_side_effects=True, vmem_limit_bytes=32 * 1024 * 1024
+            collective_id=0, has_side_effects=True, vmem_limit_bytes=60 * 1024 * 1024
         ),
     )(
         block_mask,

time: 54.4 us -> 49.8 us (0.915)
  local copies, waits for them, and re-layouts: 6.27 us -> 2.32 us
  Pallas kernels: 47.2 us -> 46.6 us
    unnamed x14 -> x4, local copies, waits for them, and re-layouts: 6.27 us -> 2.32 us
    pallas_call x1, Pallas kernels: 47.2 us -> 46.6 us  [planned(): pl.pallas_call(functools.partial(fused, rows_n, cols_n), out_shape=(jax.S...]
where the time goes in v2:
time: 49.8 us; the launch traced here: 49.6 us
  Pallas kernels  46.6 us (94%)
  local copies, waits for them, and re-layouts  2.32 us (5%)
  between operations  0.65 us (1%)
    pallas_call x1, Pallas kernels, planned(): pl.pallas_call(functools.partial(fused, rows_n, cols_n), out_shape=(jax.S...  46.6 us
    unnamed x4, local copies, waits for them, and re-layouts  2.32 us

profile of v2, /device:TPU:0, one launch (start us, length us, event | category | flops | bytes accessed | tf_op | source)
XLA Modules:
  0.0 49.6 jit_solution(12119898927499076251)
XLA Ops:
  0.6 46.6 %shard_map.77 = (f32[64,512]{1,0:T(8,128)}, f32[4,128,128]{2,1,0:T(8,128)}) custom-call(s32[8,8]{1,0:T(8,128)} %mask_hbm.1, s32[8]{0:T(128)} %ids_hbm.1, s32[4,4]{1,0:T(4,128)} %lists_hbm.1, f32[4,2,64,256]{3,2,1,0:T(8,128)} %bitcast.1, f32[64,512]{1,0:T(8,128)} %panels_hbm.1, f32[4,128,128]{2,1,0:T(8,128)} %diag_hbm.1), custom_call_target="tpu_custom_call" | custom-call | tf_op jit(solution)/shard_map/pallas_call | solution.py:364
  47.3 0.0 copy-start
  47.3 1.6 %copy.10 = f32[64,512]{1,0:T(8,128)} copy(f32[64,512]{1,0:T(8,128)} %get-tuple-element.4) | data formatting | bytes 262144
  48.9 0.0 copy-done
  48.9 0.7 %copy.11 = f32[4,128,128]{2,1,0:T(8,128)} copy(f32[4,128,128]{2,1,0:T(8,128)S(1)} %copy-done) | data formatting | bytes 524288
Async XLA Ops:
  47.3 1.6 %copy-start = (f32[4,128,128]{2,1,0:T(8,128)S(1)}, f32[4,128,128]{2,1,0:T(8,128)}, u32[]{:S(2)}) copy-start(f32[4,128,128]{2,1,0:T(8,128)} %get-tuple-element.5) | copy-start | bytes 786436

commit v3 on v2

--- a/solution.py
+++ b/solution.py
@@ -104,13 +104,30 @@
         load.start()
 
     barrier = pltpu.get_barrier_semaphore()
-    total = rows_n * cols_n
     flat = r * cols_n + c
-    for step in range(1, total):
-        other = lax.rem(flat + step, total)
+    near_steps = [(dx, dh) for dx in range(rows_n // CORES) for dh in range(2)][1:]
+    plane_steps = [(dr, dh) for dr in range(rows_n) for dh in range(2)][1:]
+
+    def greet(to_r, to_q, to_h):
         pl.semaphore_signal(
-            barrier, inc=1, device_id=(other // cols_n, other % cols_n), device_id_type=MESH
+            barrier, inc=1, device_id=(to_r, 2 * to_q + to_h), device_id_type=MESH
         )
+
+    for dr, dh in plane_steps:
+        greet(lax.rem(r + dr, rows_n), q, lax.rem(h + dh, 2))
+    for step in range(1, rows_n):
+        greet(r, lax.rem(q + step, rows_n), h)
+    apart = q != r
+
+    @pl.when(apart)
+    def _():
+        for step in range(1, rows_n):
+            greet(lax.rem(r + step, rows_n), r, h)
+            source = lax.rem(q + step, rows_n)
+
+            @pl.when(source != r)
+            def _():
+                greet(q, source, h)
 
     def active(block, k):
         hit = block_ids[block] == row_lists[k, 0]
@@ -126,7 +143,8 @@
         g, i = divmod(k, per_chunk)
         act[g, :, i * W : (i + 1) * W] = panels[:, k * W : (k + 1) * W] * keep[k]
 
-    pl.semaphore_wait(barrier, total - 1)
+    met = plane - 1 + rows_n - 1
+    pl.semaphore_wait(barrier, jnp.where(apart, met + 2 * rows_n - 3, met))
 
     def remote(src, dst, send, recv, device):
         return pltpu.make_async_remote_copy(
@@ -163,8 +181,6 @@
     swap.start()
     pending.append(swap)
 
-    near_steps = [(dx, dh) for dx in range(rows_n // CORES) for dh in range(2)][1:]
-    plane_steps = [(dr, dh) for dr in range(rows_n) for dh in range(2)][1:]
     copies = {}
 
     def split_rows(source, slot, column):
@@ -174,6 +190,9 @@
             high, low = halves(source[to] * keep_block)
             a_high[slot, to * m : (to + 1) * m] = high
             a_low[slot, to * m : (to + 1) * m] = low
+
+    loads[4].wait()
+    split_rows([near_cols[to] for to in range(rows_n)], h, c)
 
     def second(g):
         for source in range(rows_n):
@@ -215,8 +234,6 @@
 
     def multiply(g):
         if g == 0:
-            loads[4].wait()
-            split_rows([near_cols[to] for to in range(rows_n)], h, c)
             swap.wait_recv()
             split_rows([far_cols[to] for to in range(rows_n)], far_h, 2 * q + far_h)
         block = needed.at[g, :, :, :, 1 - core]

time: 49.8 us -> 49.3 us (0.990)
  Pallas kernels: 46.6 us -> 46.1 us
where the time goes in v3:
time: 49.3 us; the launch traced here: 49.1 us
  Pallas kernels  46.1 us (94%)
  local copies, waits for them, and re-layouts  2.32 us (5%)
  between operations  0.65 us (1%)
    pallas_call x1, Pallas kernels, planned(): pl.pallas_call(functools.partial(fused, rows_n, cols_n), out_shape=(jax.S...  46.1 us
    unnamed x4, local copies, waits for them, and re-layouts  2.32 us

profile of v3, /device:TPU:0, one launch (start us, length us, event | category | flops | bytes accessed | tf_op | source)
XLA Modules:
  0.0 49.1 jit_solution(18171236546816899229)
XLA Ops:
  0.6 46.1 %shard_map.77 = (f32[64,512]{1,0:T(8,128)}, f32[4,128,128]{2,1,0:T(8,128)}) custom-call(s32[8,8]{1,0:T(8,128)} %mask_hbm.1, s32[8]{0:T(128)} %ids_hbm.1, s32[4,4]{1,0:T(4,128)} %lists_hbm.1, f32[4,2,64,256]{3,2,1,0:T(8,128)} %bitcast.1, f32[64,512]{1,0:T(8,128)} %panels_hbm.1, f32[4,128,128]{2,1,0:T(8,128)} %diag_hbm.1), custom_call_target="tpu_custom_call" | custom-call | tf_op jit(solution)/shard_map/pallas_call | solution.py:381
  46.8 0.0 copy-start
  46.8 1.6 %copy.10 = f32[64,512]{1,0:T(8,128)} copy(f32[64,512]{1,0:T(8,128)} %get-tuple-element.4) | data formatting | bytes 262144
  48.4 0.0 copy-done
  48.4 0.7 %copy.11 = f32[4,128,128]{2,1,0:T(8,128)} copy(f32[4,128,128]{2,1,0:T(8,128)S(1)} %copy-done) | data formatting | bytes 524288
Async XLA Ops:
  46.8 1.6 %copy-start = (f32[4,128,128]{2,1,0:T(8,128)S(1)}, f32[4,128,128]{2,1,0:T(8,128)}, u32[]{:S(2)}) copy-start(f32[4,128,128]{2,1,0:T(8,128)} %get-tuple-element.5) | copy-start | bytes 786436
